TPU v7x, 512 devices: a whole 4x8x8 slice. The times are simulated.
512 devices in a mesh: section: 32 (over y, x), expert: 16 (over z, core).
Axes of the slice: x: 4, y: 8, z: 8, core: 2. Of those that a mesh axis runs over, the one named last changes fastest.
Arguments:
- acts: bfloat16 [32, 2, 512, 6144], P('section', None, 'expert'), may hold values from -3 to 3
- routed_expert_index: int32 [32, 2, 512, 2], P('section', None, 'expert'), may hold values from 0 to 63, all different within a row; in each aligned block of 32 rows (0 to 31, 32 to 63, ..., all dimensions but the last counted through in order) at most 2 rows name the same one
- routed_expert_scores: float32 [32, 2, 512, 2], P('section', None, 'expert'), may hold values from -0.75 to 0.75
- section_norm_scale: float32 [32, 6144], P('section'), may hold values from 0.1 to 1.9
- adapter_down_weight: bfloat16 [32, 64, 16, 6144], P('section', 'expert'), may hold values from -0.078125 to 0.078125
- adapter_up_weight: bfloat16 [32, 64, 16, 6144], P('section', 'expert'), may hold values from -1.5 to 1.5
Outputs:
- handed: bfloat16 [32, 2, 512, 6144], P('section', None, 'expert')
Inputs may be any that keep to these rules, and one draw needn't show every extreme that they name: `routed_expert_index`: within one micro-batch, the 32 tokens of one index of expert name no expert more than 2 times; a token's two experts differ.
All inputs are finite; a program needn't handle non-finite values.
Results may differ from a plain program's by a relative error of at most 0.0095.
Values may be sent and summed in bfloat16 or wider, within the bound.
A program may use at most 64 MiB of HBM per device.

v0:
```python
import jax
import jax.numpy as jnp
from jax import lax
from jax.sharding import PartitionSpec as P

TOP = 2


def shifted(block, axis, distance):
    devices = range(lax.axis_size(axis))
    route = [((i - distance) % len(devices), i) for i in devices]
    return lax.ppermute(block, axis, route)


def normalize(acts_block, gain_row):
    rows_float = acts_block.astype(jnp.float32)
    inverse = lax.rsqrt(jnp.mean(rows_float * rows_float, axis=-1, keepdims=True) + 1e-05)
    return (rows_float * inverse * gain_row[None, :]).astype(jnp.bfloat16)


def slot_table(selected_expert, experts, capacity):
    flat_ids = selected_expert.reshape(-1)
    onehot = (flat_ids[:, None] == jnp.arange(experts, dtype=jnp.int32)[None, :]).astype(jnp.int32)
    before = jnp.cumsum(onehot, axis=0) - onehot
    position = jnp.sum(before * onehot, axis=1)
    return flat_ids * capacity + position


def fill_slots(normed, slot_ids, total_slots):
    count_rows = slot_ids.shape[0]
    owners = (
        jnp.zeros((total_slots,), jnp.int32)
        .at[slot_ids]
        .set(jnp.arange(1, count_rows + 1, dtype=jnp.int32))
    )
    tokens_of = jnp.maximum(owners - 1, 0) // TOP
    picked = jnp.take(normed, tokens_of, axis=0)
    return jnp.where((owners > 0)[:, None], picked, jnp.zeros_like(picked))


def apply_down(received, down_projected_rows):
    return jnp.einsum(
        "nesd,erd->nesr", received, down_projected_rows, preferred_element_type=jnp.float32
    ).astype(jnp.bfloat16)


def apply_experts(received, down_projected_rows, up_projected_rows):
    low_rank = apply_down(received, down_projected_rows)
    return jnp.einsum(
        "nesr,erd->nesd", low_rank, up_projected_rows, preferred_element_type=jnp.float32
    ).astype(jnp.bfloat16)


def combine(acts_block, deltas, logits):
    first_gate = 1.0 / (1.0 + jnp.exp(logits[:, 1] - logits[:, 0]))
    second_gate = 1.0 / (1.0 + jnp.exp(logits[:, 0] - logits[:, 1]))
    gate_pair = jnp.stack([first_gate, second_gate], axis=1)
    mixed_rows = acts_block.astype(jnp.float32) + jnp.sum(
        gate_pair[:, :, None] * deltas.astype(jnp.float32), axis=1
    )
    return mixed_rows.astype(jnp.bfloat16)


def local(
    acts,
    routed_expert_index,
    routed_expert_scores,
    section_norm_scale,
    adapter_down_weight,
    adapter_up_weight,
):
    groups = lax.axis_size("expert")
    section_token_count = adapter_down_weight.shape[1]
    experts = section_token_count * groups
    micro_count = acts.shape[1]
    tok_rows = acts.shape[2]
    width_model = acts.shape[3]
    capacity = max(2, 3 * TOP * tok_rows // (2 * experts))
    down_projected_rows = adapter_down_weight[0]
    up_projected_rows = adapter_up_weight[0]
    gain_row = section_norm_scale[0]
    total_slots = experts * capacity
    slot_list = []
    buffers = []
    for step in range(micro_count):
        normed = normalize(acts[0, step], gain_row)
        slot_ids = slot_table(routed_expert_index[0, step], experts, capacity)
        filled = fill_slots(normed, slot_ids, total_slots)
        slot_list.append(slot_ids)
        buffers.append(filled.reshape(groups, section_token_count, capacity, width_model))
    picks = []
    for step in range(micro_count):
        returned = lax.all_to_all(
            apply_experts(
                lax.all_to_all(buffers[step], "expert", split_axis=0, concat_axis=0, tiled=True),
                down_projected_rows,
                up_projected_rows,
            ),
            "expert",
            split_axis=0,
            concat_axis=0,
            tiled=True,
        )
        last_width = returned.shape[-1]
        flat_back = returned.reshape(total_slots, last_width)
        picks.append(
            jnp.take(flat_back, slot_list[step], axis=0).reshape(tok_rows, TOP, last_width)
        )
    results = []
    for step in range(micro_count):
        mixed_rows = combine(acts[0, step], picks[step], routed_expert_scores[0, step])
        results.append(mixed_rows)
    stacked = jnp.stack(results)[None]
    stacked = shifted(stacked, "section", 1)
    return stacked


def solution(mesh):
    return jax.shard_map(
        local,
        mesh=mesh,
        in_specs=(
            P("section", None, "expert", None),
            P("section", None, "expert", None),
            P("section", None, "expert", None),
            P("section", None),
            P("section", "expert", None, None),
            P("section", "expert", None, None),
        ),
        out_specs=P("section", None, "expert", None),
        check_vma=False,
    )
```

profile of v0, /device:TPU:1, one launch (start us, length us, event | category | flops | bytes accessed | tf_op | source)
XLA Modules:
  0.0 231.5 jit_solution(10693687856366921320)
XLA Ops:
  0.0 0.0 copy-start
  0.0 0.8 fusion.50
  0.8 0.1 copy.45
  0.9 0.1 eq.34
  1.0 0.1 fusion.42
  1.0 0.1 reduce_window_sum.18
  1.1 0.2 select_reduce_fusion
  1.3 0.1 copy.46
  1.4 0.1 mul.104
  1.5 0.8 scatter_custom_fusion.1
  2.4 1.4 fusion.26
  3.8 1.4 fusion.28
  5.1 2.6 %gather_fusion.2 = bf16[128,6144]{1,0:T(8,128)(2,1)} fusion(bf16[32,6144]{1,0:T(8,128)(2,1)S(1)} %get-tuple-element.18, s32[1024]{0:T(1024)S(1)} %pad_clamp_fusion.1), kind=kCustom, calls=%fused_computation.2.clone | custom fusion | bytes 3146240 | tf_op jit(solution)/shard_map/jit(_take)/gather | solution.py:37
  7.8 1.6 select_select_fusion
  9.5 1.9 reshape.156
  11.4 11.8 %all-to-all-start.2 = ((bf16[16,4,2,6144]{3,2,1,0:T(2,128)(2,1)}), bf16[16,4,2,6144]{3,2,1,0:T(2,128)(2,1)}, u32[]{:S(2)}, u32[]{:S(2)}) async-start(bf16[16,4,2,6144]{3,2,1,0:T(2,128)(2,1)} %reshape.156), calls=%async_computation.2 | async-start | bytes 3145728 | tf_op jit(solution)/shard_map/all_to_all | solution.py:95
  23.2 0.1 copy.40
  23.3 0.1 eq.30
  23.4 0.1 fusion.43
  23.5 0.1 reduce_window_sum.17
  23.6 0.1 copy.41
  23.7 0.1 mul.92
  23.8 0.2 select_reduce_fusion.1
  24.0 0.8 scatter_custom_fusion
  24.8 2.6 %gather_fusion = bf16[128,6144]{1,0:T(8,128)(2,1)} fusion(bf16[32,6144]{1,0:T(8,128)(2,1)S(1)} %get-tuple-element.17, s32[1024]{0:T(1024)S(1)} %pad_clamp_fusion.3), kind=kCustom, calls=%fused_computation.clone | custom fusion | bytes 3146240 | tf_op jit(solution)/shard_map/jit(_take)/gather | solution.py:37
  27.4 1.6 select_select_fusion.1
  29.1 1.9 reshape.154
  31.0 30.7 %all-to-all-done.2 = bf16[16,4,2,6144]{3,2,1,0:T(2,128)(2,1)} async-done(((bf16[16,4,2,6144]{3,2,1,0:T(2,128)(2,1)}), bf16[16,4,2,6144]{3,2,1,0:T(2,128)(2,1)}, u32[]{:S(2)}, u32[]{:S(2)}) %all-to-all-start.2) | async-done | bytes 1572896 | tf_op jit(solution)/shard_map/all_to_all | solution.py:95
  61.7 4.3 %all-to-all-start = ((bf16[16,4,2,6144]{3,2,1,0:T(2,128)(2,1)}), bf16[16,4,2,6144]{3,2,1,0:T(2,128)(2,1)S(1)}, u32[]{:S(2)}, u32[]{:S(2)}) async-start(bf16[16,4,2,6144]{3,2,1,0:T(2,128)(2,1)} %reshape.154), calls=%async_computation | async-start | bytes 3145728 | tf_op jit(solution)/shard_map/all_to_all | solution.py:95
  66.0 0.0 copy-done
  66.0 0.0 copy-done.6
  66.0 4.0 %fusion.1 = bf16[16,4,2,6144]{3,0,2,1:T(8,128)(2,1)} fusion(bf16[16,4,2,6144]{3,2,1,0:T(2,128)(2,1)} %all-to-all-done.2, bf16[1,4,16,6144]{3,2,1,0:T(8,128)(2,1)S(1)} %copy-done, bf16[1,4,16,6144]{3,2,1,0:T(8,128)(2,1)S(1)} %copy-done.6), kind=kOutput, calls=%fused_computation.9 | convolution fusion | flops 51120128 | bytes 4718592 | tf_op jit(solution)/shard_map/nesr,erd->nesd/dot_general | solution.py:49
  70.0 4.2 %copy.48 = bf16[16,4,2,6144]{3,2,1,0:T(2,128)(2,1)} copy(bf16[16,4,2,6144]{3,0,2,1:T(8,128)(2,1)} %fusion.1) | data formatting | bytes 3145728 | tf_op jit(solution)/shard_map/convert_element_type | solution.py:51
  74.2 30.2 %all-to-all-done = bf16[16,4,2,6144]{3,2,1,0:T(2,128)(2,1)S(1)} async-done(((bf16[16,4,2,6144]{3,2,1,0:T(2,128)(2,1)}), bf16[16,4,2,6144]{3,2,1,0:T(2,128)(2,1)S(1)}, u32[]{:S(2)}, u32[]{:S(2)}) %all-to-all-start) | async-done | bytes 1572896 | tf_op jit(solution)/shard_map/all_to_all | solution.py:95
  104.4 1.2 copy-done.5
  105.6 4.3 %all-to-all-start.3 = ((bf16[16,4,2,6144]{3,2,1,0:T(2,128)(2,1)}), bf16[16,4,2,6144]{3,2,1,0:T(2,128)(2,1)S(1)}, u32[]{:S(2)}, u32[]{:S(2)}) async-start(bf16[16,4,2,6144]{3,2,1,0:T(2,128)(2,1)} %copy.48), calls=%async_computation.3 | async-start | bytes 3145728 | tf_op jit(solution)/shard_map/all_to_all | solution.py:93
  109.8 4.0 %fusion = bf16[16,4,2,6144]{3,0,2,1:T(8,128)(2,1)} fusion(bf16[16,4,2,6144]{3,2,1,0:T(2,128)(2,1)} %copy-done.5, bf16[1,4,16,6144]{3,2,1,0:T(8,128)(2,1)S(1)} %copy-done, bf16[1,4,16,6144]{3,2,1,0:T(8,128)(2,1)S(1)} %copy-done.6), kind=kOutput, calls=%fused_computation.8 | convolution fusion | flops 51120128 | bytes 4718592 | tf_op jit(solution)/shard_map/nesr,erd->nesd/dot_general | solution.py:49
  113.9 4.2 %copy.43 = bf16[16,4,2,6144]{3,2,1,0:T(2,128)(2,1)} copy(bf16[16,4,2,6144]{3,0,2,1:T(8,128)(2,1)} %fusion) | data formatting | bytes 3145728 | tf_op jit(solution)/shard_map/convert_element_type | solution.py:51
  118.1 30.2 %all-to-all-done.3 = bf16[16,4,2,6144]{3,2,1,0:T(2,128)(2,1)S(1)} async-done(((bf16[16,4,2,6144]{3,2,1,0:T(2,128)(2,1)}), bf16[16,4,2,6144]{3,2,1,0:T(2,128)(2,1)S(1)}, u32[]{:S(2)}, u32[]{:S(2)}) %all-to-all-start.3) | async-done | bytes 1572896 | tf_op jit(solution)/shard_map/all_to_all | solution.py:93
  148.3 1.2 copy-done.2
  149.4 4.3 %all-to-all-start.1 = ((bf16[16,4,2,6144]{3,2,1,0:T(2,128)(2,1)}), bf16[16,4,2,6144]{3,2,1,0:T(2,128)(2,1)}, u32[]{:S(2)}, u32[]{:S(2)}) async-start(bf16[16,4,2,6144]{3,2,1,0:T(2,128)(2,1)} %copy.43), calls=%async_computation.1 | async-start | bytes 3145728 | tf_op jit(solution)/shard_map/all_to_all | solution.py:93
  153.8 0.0 copy-done.7
  153.8 0.1 copy.44
  153.9 0.1 copy.39
  154.1 3.6 %reshape.157 = bf16[128,6144]{1,0:T(8,128)(2,1)S(1)} reshape(bf16[16,4,2,6144]{3,2,1,0:T(2,128)(2,1)} %copy-done.2) | data formatting | bytes 3145728 | tf_op jit(solution)/shard_map/reshape | solution.py:105
  157.6 1.0 gather_fusion.3
  158.7 0.2 select_convert_fusion
  158.8 2.1 reshape.163
  160.9 31.3 %all-to-all-done.1 = bf16[16,4,2,6144]{3,2,1,0:T(2,128)(2,1)} async-done(((bf16[16,4,2,6144]{3,2,1,0:T(2,128)(2,1)}), bf16[16,4,2,6144]{3,2,1,0:T(2,128)(2,1)}, u32[]{:S(2)}, u32[]{:S(2)}) %all-to-all-start.1) | async-done | bytes 1572896 | tf_op jit(solution)/shard_map/all_to_all | solution.py:93
  192.2 3.6 %reshape.155 = bf16[128,6144]{1,0:T(8,128)(2,1)S(1)} reshape(bf16[16,4,2,6144]{3,2,1,0:T(2,128)(2,1)} %all-to-all-done.1) | data formatting | bytes 3145728 | tf_op jit(solution)/shard_map/reshape | solution.py:105
  195.8 1.0 gather_fusion.1
  196.8 1.3 select_convert_fusion.1
  198.2 3.3 %reshape.160 = f32[32,2,6144]{2,1,0:T(2,128)} reshape(f32[64,6144]{1,0:T(8,128)} %select_convert_fusion.1) | data formatting | bytes 3145728 | tf_op jit(solution)/shard_map/convert_element_type | solution.py:59
  201.4 0.0 copy-done.3
  201.4 2.1 multiply_reduce_fusion
  203.5 0.0 copy-done.4
  203.5 0.0 copy-start.1
  203.5 2.1 multiply_reduce_fusion.1
  205.6 0.0 copy-done.1
  205.6 0.1 fusion.30
  205.7 0.1 maximum_bitcast_fusion
  205.8 3.1 %collective-permute-start = (bf16[1,2,32,6144]{3,2,1,0:T(8,128)(2,1)S(1)}, bf16[1,2,32,6144]{3,2,1,0:T(8,128)(2,1)S(1)}, u32[]{:S(2)}, u32[]{:S(2)}) collective-permute-start(bf16[1,2,32,6144]{3,2,1,0:T(8,128)(2,1)S(1)} %maximum_bitcast_fusion), channel_id=1, source_target_pairs={{496,0},{0,16},{16,32},{32,48},{48,64},{64,80},{80,96},{96,112},{1... | collective-permute-start | bytes 2359304 | tf_op jit(solution)/shard_map/ppermute | solution.py:12
  208.9 21.7 %collective-permute-done = bf16[1,2,32,6144]{3,2,1,0:T(8,128)(2,1)S(1)} collective-permute-done((bf16[1,2,32,6144]{3,2,1,0:T(8,128)(2,1)S(1)}, bf16[1,2,32,6144]{3,2,1,0:T(8,128)(2,1)S(1)}, u32[]{:S(2)}, u32[]{:S(2)}) %collective-permute-start) | collective-permute-done | bytes 786464 | tf_op jit(solution)/shard_map/ppermute | solution.py:12
  230.6 0.9 copy.68
  (22 shorter events, 0.1 us)
Async XLA Ops:
  0.0 66.0 %copy-start = (bf16[1,4,16,6144]{3,2,1,0:T(8,128)(2,1)S(1)}, bf16[1,4,16,6144]{3,2,1,0:T(8,128)(2,1)}, u32[]{:S(2)}) copy-start(bf16[1,4,16,6144]{3,2,1,0:T(8,128)(2,1)} %param.15) | copy-start | bytes 2359300
  11.4 50.4 %all-to-all-start.2 = ((bf16[16,4,2,6144]{3,2,1,0:T(2,128)(2,1)}), bf16[16,4,2,6144]{3,2,1,0:T(2,128)(2,1)}, u32[]{:S(2)}, u32[]{:S(2)}) async-start(bf16[16,4,2,6144]{3,2,1,0:T(2,128)(2,1)} %reshape.156), calls=%async_computation.2 | async-start | bytes 3145728 | tf_op jit(solution)/shard_map/all_to_all | solution.py:95
  31.0 35.0 %copy-start.6 = (bf16[1,4,16,6144]{3,2,1,0:T(8,128)(2,1)S(1)}, bf16[1,4,16,6144]{3,2,1,0:T(8,128)(2,1)}, u32[]{:S(2)}) copy-start(bf16[1,4,16,6144]{3,2,1,0:T(8,128)(2,1)} %param.14) | copy-start | bytes 2359300
  61.7 42.7 %all-to-all-start = ((bf16[16,4,2,6144]{3,2,1,0:T(2,128)(2,1)}), bf16[16,4,2,6144]{3,2,1,0:T(2,128)(2,1)S(1)}, u32[]{:S(2)}, u32[]{:S(2)}) async-start(bf16[16,4,2,6144]{3,2,1,0:T(2,128)(2,1)} %reshape.154), calls=%async_computation | async-start | bytes 3145728 | tf_op jit(solution)/shard_map/all_to_all | solution.py:95
  104.4 1.2 copy-start.5
  105.6 42.7 %all-to-all-start.3 = ((bf16[16,4,2,6144]{3,2,1,0:T(2,128)(2,1)}), bf16[16,4,2,6144]{3,2,1,0:T(2,128)(2,1)S(1)}, u32[]{:S(2)}, u32[]{:S(2)}) async-start(bf16[16,4,2,6144]{3,2,1,0:T(2,128)(2,1)} %copy.48), calls=%async_computation.3 | async-start | bytes 3145728 | tf_op jit(solution)/shard_map/all_to_all | solution.py:93
  118.1 35.7 %copy-start.7 = (f32[1,2,32,2]{2,3,1,0:T(2,128)S(1)}, f32[1,2,32,2]{2,3,1,0:T(2,128)}, u32[]{:S(2)}) copy-start(f32[1,2,32,2]{2,3,1,0:T(2,128)} %param.12) | copy-start | bytes 1540
  148.3 1.2 copy-start.2
  149.4 42.8 %all-to-all-start.1 = ((bf16[16,4,2,6144]{3,2,1,0:T(2,128)(2,1)}), bf16[16,4,2,6144]{3,2,1,0:T(2,128)(2,1)}, u32[]{:S(2)}, u32[]{:S(2)}) async-start(bf16[16,4,2,6144]{3,2,1,0:T(2,128)(2,1)} %copy.43), calls=%async_computation.1 | async-start | bytes 3145728 | tf_op jit(solution)/shard_map/all_to_all | solution.py:93
  198.2 3.3 %copy-start.3 = (f32[32,2,6144]{2,1,0:T(2,128)S(1)}, f32[32,2,6144]{2,1,0:T(2,128)}, u32[]{:S(2)}) copy-start(f32[32,2,6144]{2,1,0:T(2,128)} %reshape.163) | copy-start | bytes 4718596
  201.4 2.1 copy-start.4
  203.5 2.1 copy-start.1
  205.8 24.8 %collective-permute-start = (bf16[1,2,32,6144]{3,2,1,0:T(8,128)(2,1)S(1)}, bf16[1,2,32,6144]{3,2,1,0:T(8,128)(2,1)S(1)}, u32[]{:S(2)}, u32[]{:S(2)}) collective-permute-start(bf16[1,2,32,6144]{3,2,1,0:T(8,128)(2,1)S(1)} %maximum_bitcast_fusion), channel_id=1, source_target_pairs={{496,0},{0,16},{16,32},{32,48},{48,64},{64,80},{80,96},{96,112},{1... | collective-permute-start | bytes 2359304 | tf_op jit(solution)/shard_map/ppermute | solution.py:12
where the time goes:
time: 232 us; the launch traced here: 231 us
  waiting for transfers between devices  144 us (62%)
  local copies, waits for them, and re-layouts  37.7 us (16%)
  starting transfers between devices  27.8 us (12%)
  other arithmetic  13.5 us (6%)
  matrix products  8.06 us (3%)
    all_to_all x2, waiting for transfers between devices, local(): lax.all_to_all(apply_experts(lax.all_to_all(buffers[step], 'expert', spli...  61.5 us
    all_to_all x2, waiting for transfers between devices, local(): lax.all_to_all(buffers[step], 'expert', split_axis=0, concat_axis=0, tile...  60.9 us
    ppermute x1, waiting for transfers between devices, shifted(): return lax.ppermute(block, axis, route)  21.7 us
    all_to_all x2, starting transfers between devices, local(): lax.all_to_all(buffers[step], 'expert', split_axis=0, concat_axis=0, tile...  16.1 us
    all_to_all x2, starting transfers between devices, local(): lax.all_to_all(apply_experts(lax.all_to_all(buffers[step], 'expert', spli...  8.57 us
    convert_element_type x2, local copies, waits for them, and re-layouts, apply_experts(): return jnp.einsum('nesr,erd->nesd', low_rank, up_projected_rows, preferre...  8.36 us
    dot_general x2, matrix products, apply_experts(): jnp.einsum('nesr,erd->nesd', low_rank, up_projected_rows, preferred_eleme...  8.06 us
    reshape x2, local copies, waits for them, and re-layouts, local(): flat_back = returned.reshape(total_slots, last_width)  7.12 us
  transfers between devices with their start and end apart: 5, of which 5 were waited for; matrix products, arithmetic and copies ran while one was open for 14% of the time, Pallas kernels for 0%

commit v1 on v0

v1 whole, which is shorter than its diff:
```python
import jax
import jax.numpy as jnp
from jax import lax
from jax.experimental import pallas as pl
from jax.experimental.pallas import tpu as pltpu
from jax.sharding import PartitionSpec as P

MESH = pl.DeviceIdType.MESH
SECTIONS = 32
CHIPS = 8
GROUP = 16
MB = 2
TOK = 32
RANK = 16
LOCAL_EXPERTS = 4
WIDTH = 6144
SLICE = WIDTH // GROUP
BLOCK = 2 * MB * TOK
F32 = jnp.float32
BF16 = jnp.bfloat16


def kernel(
    acts,
    index,
    scores,
    gain,
    down,
    up,
    out,
    own_acts,
    acts_in,
    down_in,
    up_in,
    flat,
    meta,
    part,
    red,
    low,
    mixed,
    send_out,
    hand,
    local_sem,
    acts_ss,
    acts_rs,
    down_ss,
    down_rs,
    up_ss,
    up_rs,
    meta_ss,
    meta_rs,
    part_ss,
    part_rs,
    low_ss,
    low_rs,
    out_ss,
    out_rs,
    hand_ss,
    hand_rs,
):
    s = lax.axis_index("section")
    e = lax.axis_index("expert")
    z = e // 2
    c = lax.rem(e, 2)
    s_next = lax.rem(s + 1, SECTIONS)
    s_prev = lax.rem(s + SECTIONS - 1, SECTIONS)

    def hop(j):
        return 4 + ((j + 1) // 2) * (1 - 2 * lax.rem(j, 2))

    def peer(i):
        return lax.rem(z + hop(i // 2), CHIPS) * 2 + lax.rem(c + 1 - lax.rem(i, 2), 2)

    def source(i):
        return lax.rem(z + CHIPS - hop(i // 2), CHIPS) * 2 + lax.rem(c + 1 - lax.rem(i, 2), 2)

    def lanes(k, width):
        return pl.ds(pl.multiple_of(k * width, width), width)

    def each(count, body):
        def step(i, carry):
            body(i)
            return carry

        lax.fori_loop(0, count, step, 0)

    barrier = pltpu.get_barrier_semaphore()

    def greet(i):
        pl.semaphore_signal(barrier, inc=1, device_id=(s, peer(i)), device_id_type=MESH)

    each(15, greet)
    pl.semaphore_signal(barrier, inc=1, device_id=(s_prev, e), device_id_type=MESH)
    pl.semaphore_wait(barrier, 16)

    def remote(src, dst, ss, rs, section, device):
        return pltpu.make_async_remote_copy(
            src_ref=src,
            dst_ref=dst,
            send_sem=ss,
            recv_sem=rs,
            device_id=(section, device),
            device_id_type=MESH,
        )

    def acts_copy(i, device, slot):
        return remote(
            acts.at[0, :, :, lanes(device, SLICE)], acts_in.at[slot], acts_ss.at[i], acts_rs.at[i], s, device
        )

    def down_copy(i, device, slot):
        return remote(
            down.at[0, :, :, lanes(device, SLICE)], down_in.at[slot], down_ss.at[i], down_rs.at[i], s, device
        )

    def up_copy(i, device, slot):
        return remote(up.at[0, :, :, lanes(device, SLICE)], up_in.at[slot], up_ss.at[i], up_rs.at[i], s, device)

    def meta_copy(i, device, slot):
        return remote(meta.at[slot], meta.at[slot], meta_ss.at[i], meta_rs.at[i], s, device)

    def part_copy(i, device, slot):
        return remote(
            part.at[lax.rem(device, 2), :, lanes(device // 2, BLOCK)],
            red.at[slot],
            part_ss.at[i],
            part_rs.at[i],
            s,
            device,
        )

    def low_copy(i, device, slot):
        return remote(low.at[slot], low.at[slot], low_ss.at[i], low_rs.at[i], s, device)

    def out_copy(i, device, slot):
        return remote(
            send_out.at[device], hand.at[slot], out_ss.at[i], out_rs.at[i], s, device
        )

    def hand_copy(i, slot):
        return remote(
            hand.at[slot],
            out.at[0, :, :, lanes(slot, SLICE)],
            hand_ss.at[i],
            hand_rs.at[i],
            s_next,
            e,
        )

    own = pltpu.make_async_copy(acts.at[0], own_acts, local_sem.at[0])
    own.start()

    def send_acts_down(i):
        acts_copy(i, peer(i), e).start()

    each(15, send_acts_down)

    def send_down(i):
        down_copy(i, peer(i), e).start()

    each(15, send_down)
    locals_ = [
        pltpu.make_async_copy(acts.at[0, :, :, lanes(e, SLICE)], acts_in.at[e], local_sem.at[1]),
        pltpu.make_async_copy(down.at[0, :, :, lanes(e, SLICE)], down_in.at[e], local_sem.at[2]),
        pltpu.make_async_copy(up.at[0, :, :, lanes(e, SLICE)], up_in.at[e], local_sem.at[3]),
    ]
    for copy in locals_:
        copy.start()

    own.wait()
    rows = MB * TOK

    def square(k, total):
        block = own_acts[:, :, lanes(k, SLICE)].astype(F32).reshape(rows, SLICE)
        return total + block * block

    squares = lax.fori_loop(0, GROUP, square, jnp.zeros((rows, SLICE), F32))
    inverse = lax.rsqrt(jnp.sum(squares, axis=1, keepdims=True) * (1.0 / WIDTH) + 1e-05)
    logits = scores[0].reshape(rows, 2)
    chosen = index[0].reshape(rows, 2).astype(F32)
    first = inverse / (1.0 + jnp.exp(logits[:, 1:2] - logits[:, 0:1]))
    second = inverse / (1.0 + jnp.exp(logits[:, 0:1] - logits[:, 1:2]))
    column = lax.broadcasted_iota(jnp.int32, (rows, 128), 1)
    table = jnp.where(
        column == 0,
        chosen[:, 0:1],
        jnp.where(
            column == 1,
            chosen[:, 1:2],
            jnp.where(column == 2, first, jnp.where(column == 3, second, 0.0)),
        ),
    )
    flat[...] = jnp.zeros_like(flat)
    flat[pl.ds(pl.multiple_of(c * rows, rows), rows), :] = table
    meta[e] = jnp.transpose(flat[...])[0:8]

    def send_meta(i):
        meta_copy(i, peer(i), e).start()

    each(15, send_meta)

    def send_up(i):
        up_copy(i, peer(i), e).start()

    each(15, send_up)

    for copy in locals_:
        copy.wait()

    def take(copy):
        def body(i):
            copy(i, source(i), source(i)).wait_recv()

        return body

    def receive(copy, dev_dependent=True):
        def body(i):
            copy(i, peer(i), source(i)).wait_recv()

        each(15, body)

    receive(acts_copy)
    receive(down_copy)
    receive(meta_copy)

    gain_row = gain[0:1, lanes(e, SLICE)]

    def down_step(n, carry):
        tokens = acts_in[pl.ds(n * 4, 4)].reshape(256, SLICE).astype(F32)
        scaled = (tokens * gain_row).astype(BF16)
        ids = []
        for k in range(2):
            parts = []
            for h in range(2):
                both = meta[4 * n + 2 * h] + meta[4 * n + 2 * h + 1]
                parts.append(both[k : k + 1])
            ids.append(jnp.concatenate(parts, axis=1))
        picked = [jnp.zeros((RANK, 256), F32) for _ in range(2)]
        for m in range(4):
            block = down_in[4 * m : 4 * m + 4].reshape(256, SLICE)
            product = lax.dot_general(
                block, scaled, (((1,), (1,)), ((), ())), preferred_element_type=F32
            )
            for g in range(16):
                piece = product[g * RANK : (g + 1) * RANK]
                expert = float(m * 16 + g)
                for k in range(2):
                    picked[k] = jnp.where(ids[k] == expert, piece, picked[k])
        for k in range(2):
            part[k, :, lanes(n, 256)] = picked[k]
        return carry

    lax.fori_loop(0, 4, down_step, 0)

    def send_part(i):
        part_copy(i, peer(i), e).start()

    each(15, send_part)
    red[e] = part[c, :, lanes(z, BLOCK)]
    receive(part_copy)

    total = red[0]
    for k in range(1, GROUP):
        total = total + red[k]
    both = meta[2 * z] + meta[2 * z + 1]
    factor = jnp.where(c == 0, both[2:3], both[3:4])
    low[e] = (total * factor).astype(BF16)

    def send_low(i):
        low_copy(i, peer(i), e).start()

    each(15, send_low)
    receive(low_copy)

    def mix_step(q, carry):
        both = meta[2 * q] + meta[2 * q + 1]
        lows = [low[2 * q].astype(F32), low[2 * q + 1].astype(F32)]
        for g in range(8):
            pieces = []
            for h in range(8):
                expert = float(g * 8 + h)
                piece = jnp.where(both[1:2] == expert, lows[1], 0.0)
                pieces.append(jnp.where(both[0:1] == expert, lows[0], piece))
            square_block = jnp.concatenate(pieces, axis=0)
            mixed[q, :, g * 128 : (g + 1) * 128] = jnp.transpose(square_block).astype(BF16)
        return carry

    lax.fori_loop(0, CHIPS, mix_step, 0)

    receive(up_copy)

    def out_block(q):
        weights = up_in[...].reshape(GROUP * LOCAL_EXPERTS * RANK, SLICE)
        delta = jnp.dot(mixed[q], weights, preferred_element_type=F32)
        base = acts_in[pl.ds(2 * q, 2)].reshape(BLOCK, SLICE).astype(F32)
        send_out[pl.ds(2 * q, 2)] = (base + delta).astype(BF16).reshape(2, MB, TOK, SLICE)

    def forward(i):
        out_copy(i, peer(i), source(i)).wait_recv()
        hand_copy(i, source(i)).start()

    def out_step(j, carry):
        out_block(lax.rem(z + hop(j), CHIPS))
        out_copy(2 * j, peer(2 * j), e).start()
        out_copy(2 * j + 1, peer(2 * j + 1), e).start()
        return carry

    def out_forward_step(j, carry):
        out_step(j, carry)
        forward(2 * j - 4)
        forward(2 * j - 3)
        return carry

    lax.fori_loop(0, 2, out_step, 0)
    lax.fori_loop(2, 7, out_forward_step, 0)
    out_block(z)
    out_copy(14, peer(14), e).start()
    own_hand = remote(
        send_out.at[e], out.at[0, :, :, lanes(e, SLICE)], hand_ss.at[15], hand_rs.at[15], s_next, e
    )
    own_hand.start()
    lax.fori_loop(10, 15, lambda i, carry: (forward(i), carry)[1], 0)

    def drain(i):
        acts_copy(i, peer(i), e).wait_send()
        down_copy(i, peer(i), e).wait_send()
        up_copy(i, peer(i), e).wait_send()
        meta_copy(i, peer(i), e).wait_send()
        part_copy(i, peer(i), e).wait_send()
        low_copy(i, peer(i), e).wait_send()
        out_copy(i, peer(i), e).wait_send()
        hand_copy(i, source(i)).wait()

    each(15, drain)
    own_hand.wait()


def local(acts, index, scores, gain, down, up):
    dma = pltpu.SemaphoreType.DMA((16,))
    any_spec = pl.BlockSpec(memory_space=pl.ANY)
    vmem_spec = pl.BlockSpec(memory_space=pltpu.VMEM)
    return pl.pallas_call(
        kernel,
        out_shape=jax.ShapeDtypeStruct(acts.shape, acts.dtype),
        in_specs=[any_spec, vmem_spec, vmem_spec, vmem_spec, any_spec, any_spec],
        out_specs=any_spec,
        scratch_shapes=[
            pltpu.VMEM((MB, TOK, WIDTH), BF16),
            pltpu.VMEM((GROUP, MB, TOK, SLICE), BF16),
            pltpu.VMEM((GROUP, LOCAL_EXPERTS, RANK, SLICE), BF16),
            pltpu.VMEM((GROUP, LOCAL_EXPERTS, RANK, SLICE), BF16),
            pltpu.VMEM((128, 128), F32),
            pltpu.VMEM((GROUP, 8, 128), F32),
            pltpu.VMEM((2, RANK, GROUP * MB * TOK), F32),
            pltpu.VMEM((GROUP, RANK, BLOCK), F32),
            pltpu.VMEM((GROUP, RANK, BLOCK), BF16),
            pltpu.VMEM((CHIPS, BLOCK, GROUP * LOCAL_EXPERTS * RANK), BF16),
            pltpu.VMEM((GROUP, MB, TOK, SLICE), BF16),
            pltpu.VMEM((GROUP, MB, TOK, SLICE), BF16),
        ]
        + [dma] * 17,
        compiler_params=pltpu.CompilerParams(
            collective_id=0, has_side_effects=True, vmem_limit_bytes=40 << 20
        ),
        cost_estimate=pl.CostEstimate(
            flops=4 * 1024 * 1024 * SLICE, bytes_accessed=4 * 786432, transcendentals=0
        ),
        name="relay",
    )(acts, index, scores, gain, down, up)


def solution(mesh):
    return jax.shard_map(
        local,
        mesh=mesh,
        in_specs=(
            P("section", None, "expert", None),
            P("section", None, "expert", None),
            P("section", None, "expert", None),
            P("section", None),
            P("section", "expert", None, None),
            P("section", "expert", None, None),
        ),
        out_specs=P("section", None, "expert", None),
        check_vma=False,
    )
```

time: 232 us -> 117 us (0.50)
  waiting for transfers between devices: 144 us -> 0 us
  Pallas kernels: 0 us -> 111 us
  local copies, waits for them, and re-layouts: 37.7 us -> 5.8 us
  starting transfers between devices: 27.8 us -> 0 us
  other arithmetic: 13.5 us -> 0 us
  matrix products: 8.06 us -> 0 us
    all_to_all x4 -> x0, waiting for transfers between devices: 122 us -> none  [the longest x2 61.5 us: local(): lax.all_to_all(apply_experts(lax.all_to_all(buffers[step], 'expert', spli...]
    pallas_call x0 -> x1, Pallas kernels: none -> 111 us  [local(): pl.pallas_call(kernel, out_shape=jax.ShapeDtypeStruct(acts.shape, acts.dt...]
    all_to_all x4 -> x0, starting transfers between devices: 24.7 us -> none  [the longest x2 16.1 us: local(): lax.all_to_all(buffers[step], 'expert', split_axis=0, concat_axis=0, tile...]
    ppermute x1 -> x0, waiting for transfers between devices: 21.7 us -> none  [shifted(): return lax.ppermute(block, axis, route)]
    convert_element_type x4 -> x0, local copies, waits for them, and re-layouts: 13.7 us -> none  [the longest x2 8.36 us: apply_experts(): return jnp.einsum('nesr,erd->nesd', low_rank, up_projected_rows, preferre...]
    reshape x4 -> x0, local copies, waits for them, and re-layouts: 11 us -> none  [the longest x2 7.12 us: local(): flat_back = returned.reshape(total_slots, last_width)]
    dot_general x2 -> x0, matrix products: 8.06 us -> none  [apply_experts(): jnp.einsum('nesr,erd->nesd', low_rank, up_projected_rows, preferred_eleme...]
    gather x4 -> x0, local copies, waits for them, and re-layouts: 7.33 us -> none  [the longest x2 5.29 us: fill_slots(): picked = jnp.take(normed, tokens_of, axis=0)]
  transfers between devices with their start and end apart: 5 -> 0, of which waited for: 5 -> 0; matrix products, arithmetic and copies ran while one was open for 14% -> 0% of each run, Pallas kernels for 0% -> 0%
where the time goes in v1:
time: 117 us
  Pallas kernels  111 us (95%)
  local copies, waits for them, and re-layouts  5.8 us (5%)
    pallas_call x1, Pallas kernels, local(): pl.pallas_call(kernel, out_shape=jax.ShapeDtypeStruct(acts.shape, acts.dt...  111 us
    unnamed x13, local copies, waits for them, and re-layouts  5.8 us

profile of v1, /device:TPU:1, one launch (start us, length us, event | category | flops | bytes accessed | tf_op | source)
XLA Modules:
  0.0 117.1 jit_solution(470048901511520236)
XLA Ops:
  0.0 0.0 copy-start.4
  0.0 0.8 copy.7.index
  0.8 0.0 copy-done.4
  0.8 0.0 copy-start.3
  0.8 0.1 copy.8.scores
  0.9 0.6 copy-done.3
  1.5 0.0 copy-start
  1.5 1.1 copy-done
  2.7 0.0 copy-start.1
  2.7 1.1 copy-done.1
  3.8 0.0 copy-start.2
  3.8 1.1 copy-done.2
  4.9 111.2 %relay.1 = bf16[1,2,32,6144]{3,2,1,0:T(8,128)(2,1)S(1)} custom-call(bf16[1,2,32,6144]{3,2,1,0:T(8,128)(2,1)S(1)} %copy-done, s32[1,2,32,2]{3,2,1,0:T(8,128)S(1)} %copy.7.index, f32[1,2,32,2]{3,2,1,0:T(8,128)S(1)} %copy.8.scores, f32[1,6144]{1,0:T(1,128)S(1)} %copy-done.3, bf16[1,4,16,6144]{3,2,1,0:T(8,128)(2,1)S(1)} %copy-done.1, ...), custom_call_target="tpu_custom_call" | custom-call | flops 1610612736 | bytes 3145728 | tf_op jit(solution)/shard_map/relay/pallas_call | solution.py:342
  116.2 0.9 copy.10
Async XLA Ops:
  0.0 0.8 copy-start.4
  0.8 0.7 copy-start.3
  1.5 1.1 copy-start
  2.7 1.1 copy-start.1
  3.8 1.1 copy-start.2

commit v2 on v0

v2 whole, which is shorter than its diff:
```python
import jax
import jax.numpy as jnp
from jax import lax
from jax.experimental import pallas as pl
from jax.experimental.pallas import tpu as pltpu
from jax.sharding import PartitionSpec as P

MESH = pl.DeviceIdType.MESH
SECTIONS = 32
CHIPS = 8
GROUP = 16
MB = 2
TOK = 32
ROWS = MB * TOK
RANK = 16
LOCAL_EXPERTS = 4
EXPERTS = GROUP * LOCAL_EXPERTS
WIDTH = 6144
SLICE = WIDTH // GROUP
LANES = 128
PARTS = SLICE // LANES
BLOCK = 2 * ROWS
ORDER = (
    (4, 1), (1, 0), (7, 0), (3, 1), (5, 1), (2, 0), (6, 0), (4, 0),
    (3, 0), (5, 0), (1, 1), (7, 1), (2, 1), (6, 1), (0, 1),
)
NEAR = (0, 1, 7, 2, 6, 3, 5, 4)
WINDOW = 8
PAIRS = ((0, 1), (7, 2), (6, 3), (5, 4))
F32 = jnp.float32
BF16 = jnp.bfloat16


def kernel(
    acts,
    index,
    scores,
    gain,
    down,
    up,
    out,
    own_acts,
    acts_in,
    down_in,
    up_in,
    gain_in,
    index_in,
    scores_in,
    place,
    flat,
    ids_in,
    gates_in,
    part,
    red,
    low,
    mixed,
    send_out,
    hand,
    local_sem,
    acts_ss,
    acts_rs,
    down_ss,
    down_rs,
    up_ss,
    up_rs,
    ids_ss,
    ids_rs,
    gates_ss,
    gates_rs,
    part_ss,
    part_rs,
    low_ss,
    low_rs,
    out_ss,
    out_rs,
    hand_ss,
    hand_rs,
):
    s = lax.axis_index("section")
    e = lax.axis_index("expert")
    z = e // 2
    c = lax.rem(e, 2)
    sibling = 2 * z + 1 - c
    s_next = lax.rem(s + 1, SECTIONS)
    s_prev = lax.rem(s + SECTIONS - 1, SECTIONS)

    others = [lax.rem(z + hops, CHIPS) * 2 + lax.rem(c + flip, 2) for hops, flip in ORDER]
    arrivals = [sibling]
    for hops in NEAR[1:]:
        other = lax.rem(z + hops, CHIPS) * 2
        arrivals += [other + 1 - c, other + c]

    def span(k, width):
        return pl.ds(pl.multiple_of(k * width, width), width)

    def piece(device, g):
        return pl.ds(pl.multiple_of(device * SLICE + g * LANES, LANES), LANES)

    def each(count, body):
        def step(i, carry):
            body(i)
            return carry

        lax.fori_loop(0, count, step, 0)

    def peers(body):
        for device in others:
            body(device)

    barrier = pltpu.get_barrier_semaphore()

    def greet(device):
        pl.semaphore_signal(barrier, inc=1, device_id=(s, device), device_id_type=MESH)

    peers(greet)
    pl.semaphore_signal(barrier, inc=1, device_id=(s_prev, e), device_id_type=MESH)

    early = [
        pltpu.make_async_copy(acts, own_acts, local_sem.at[0]),
        pltpu.make_async_copy(index.at[0], index_in, local_sem.at[1]),
        pltpu.make_async_copy(scores.at[0], scores_in, local_sem.at[2]),
    ]
    late = [
        pltpu.make_async_copy(gain.at[:, span(e, SLICE)], gain_in, local_sem.at[3]),
        pltpu.make_async_copy(acts.at[:, span(e, SLICE)], acts_in.at[e], local_sem.at[4]),
        pltpu.make_async_copy(down.at[:, span(e, SLICE)], down_in.at[e], local_sem.at[5]),
    ]
    for g in range(PARTS):
        late.append(pltpu.make_async_copy(up.at[:, piece(e, g)], up_in.at[g, e], local_sem.at[6 + g]))
    for copy in early + late:
        copy.start()
    place[...] = jnp.zeros_like(place)
    flat[...] = jnp.zeros_like(flat)

    for copy in early:
        copy.wait()
    for m in range(MB):
        place[m, 0:2, 0:TOK] = index_in[m].astype(F32)
        place[m, 2:4, 0:TOK] = scores_in[m]
    placed = pltpu.roll(place[0], c * ROWS, 1) + pltpu.roll(place[1], c * ROWS + TOK, 1)
    ids_in[e] = placed[0:2]

    def square(k, total):
        block = own_acts[:, span(k, SLICE)].astype(F32)
        return total + block * block

    squares = lax.fori_loop(0, GROUP, square, jnp.zeros((ROWS, SLICE), F32))
    inverse = lax.rsqrt(jnp.sum(squares, axis=1, keepdims=True) * (1.0 / WIDTH) + 1e-05)
    flat[span(c, ROWS), :] = jnp.broadcast_to(inverse, (ROWS, LANES))
    inverse_row = jnp.transpose(flat[...])[0:1]
    first = inverse_row / (1.0 + jnp.exp(placed[3:4] - placed[2:3]))
    second = inverse_row / (1.0 + jnp.exp(placed[2:3] - placed[3:4]))
    gates_in[c] = jnp.concatenate([first, second], axis=0)
    pl.semaphore_wait(barrier, GROUP)

    def remote(src, dst, ss, rs, section, device):
        return pltpu.make_async_remote_copy(
            src_ref=src,
            dst_ref=dst,
            send_sem=ss,
            recv_sem=rs,
            device_id=(section, device),
            device_id_type=MESH,
        )

    def acts_copy(device, slot):
        src = acts.at[:, span(device, SLICE)]
        return remote(src, acts_in.at[slot], acts_ss.at[device], acts_rs.at[slot], s, device)

    def down_copy(device, slot):
        src = down.at[:, span(device, SLICE)]
        return remote(src, down_in.at[slot], down_ss.at[device], down_rs.at[slot], s, device)

    def up_copy(g):
        def copy(device, slot):
            src = up.at[:, piece(device, g)]
            return remote(src, up_in.at[g, slot], up_ss.at[g, device], up_rs.at[g, slot], s, device)

        return copy

    def ids_copy(device, slot):
        return remote(ids_in.at[slot], ids_in.at[slot], ids_ss.at[device], ids_rs.at[slot], s, device)

    def gates_copy(slot):
        return remote(
            gates_in.at[slot], gates_in.at[slot], gates_ss, gates_rs, s, sibling
        )

    def part_copy(device, slot):
        src = part.at[lax.rem(device, 2), :, span(device // 2, BLOCK)]
        return remote(src, red.at[slot], part_ss.at[device], part_rs.at[slot], s, device)

    def low_copy(device, slot):
        return remote(low.at[slot], low.at[slot], low_ss.at[device], low_rs.at[slot], s, device)

    def out_copy(g):
        def copy(device, slot):
            return remote(
                send_out.at[g, device], hand.at[g, slot], out_ss.at[g, device], out_rs.at[g, slot], s, device
            )

        return copy

    def hand_copy(g, slot, own):
        src = send_out if own else hand
        return remote(
            src.at[g, slot],
            out.at[:, piece(slot, g)],
            hand_ss.at[g, slot],
            hand_rs.at[g, slot],
            s_next,
            e,
        )

    def send(copy):
        peers(lambda device: copy(device, e).start())

    def sent(copy):
        peers(lambda device: copy(device, e).wait_send())

    def received(copy):
        peers(lambda device: copy(device, device).wait_recv())

    gates_copy(c).start()
    send(ids_copy)
    bulk = [acts_copy(device, e) for device in others] + [down_copy(device, e) for device in others]
    for k, copy in enumerate(bulk):
        if k >= WINDOW:
            bulk[k - WINDOW].wait_send()
        copy.start()
    G0 = 3
    for k, copy in enumerate(bulk[-WINDOW:]):
        copy.wait_send()
        for device in others[G0 * k : G0 * (k + 1)]:
            up_copy(0)(device, e).start()
    for device in others[G0 * WINDOW :]:
        up_copy(0)(device, e).start()


    for copy in late:
        copy.wait()
    received(ids_copy)
    received(acts_copy)
    received(down_copy)

    def pick_block(n):
        tokens = acts_in[span(n, 4)].reshape(2 * BLOCK, SLICE).astype(F32)
        scaled = (tokens * gain_in[...]).astype(BF16)
        halves = [ids_in[4 * n + 2 * h] + ids_in[4 * n + 2 * h + 1] for h in range(2)]
        both = jnp.concatenate(halves, axis=1)
        picked = [jnp.zeros((RANK, 2 * BLOCK), F32) for _ in range(2)]
        for m in range(4):
            block = down_in[4 * m : 4 * m + 4].reshape(256, SLICE)
            product = lax.dot_general(block, scaled, (((1,), (1,)), ((), ())), preferred_element_type=F32)
            for g in range(16):
                rows = product[g * RANK : (g + 1) * RANK]
                for k in range(2):
                    picked[k] = jnp.where(both[k : k + 1] == float(m * 16 + g), rows, picked[k])
        for k in range(2):
            part[k, :, span(n, 2 * BLOCK)] = picked[k]

    def pick_step(i):
        n = lax.rem(z // 2 + 1 + i, 4)
        pick_block(n)
        for h in range(4):
            part_copy(4 * n + h, e).start()

    each(3, pick_step)
    pick_block(z // 2)
    chip = z + 1 - 2 * lax.rem(z, 2)
    part_copy(2 * chip, e).start()
    part_copy(2 * chip + 1, e).start()
    part_copy(sibling, e).start()
    red[e] = part[c, :, span(z, BLOCK)]
    send(up_copy(1))
    received(part_copy)
    gates_copy(1 - c).wait_recv()

    total = red[0]
    for k in range(1, GROUP):
        total = total + red[k]
    gates = gates_in[0] + gates_in[1]
    low[e] = (total * jnp.where(c == 0, gates[0:1], gates[1:2])).astype(BF16)
    send(low_copy)
    send(up_copy(2))
    received(low_copy)


    def mix_step(q):
        both = ids_in[2 * q] + ids_in[2 * q + 1]
        lows = [low[2 * q].astype(F32), low[2 * q + 1].astype(F32)]
        for g in range(8):
            pieces = []
            for h in range(8):
                expert = float(g * 8 + h)
                rows = jnp.where(both[1:2] == expert, lows[1], 0.0)
                pieces.append(jnp.where(both[0:1] == expert, lows[0], rows))
            tile = jnp.concatenate(pieces, axis=0)
            mixed[q, :, g * LANES : (g + 1) * LANES] = jnp.transpose(tile).astype(BF16)

    each(CHIPS, mix_step)

    def out_part(g):
        received(up_copy(g))
        weights = up_in[g].reshape(EXPERTS * RANK, LANES)
        for pair in PAIRS:
            chips = [lax.rem(z + hops, CHIPS) for hops in pair]
            rows = jnp.concatenate([mixed[q] for q in chips], axis=0)
            delta = jnp.dot(rows, weights, preferred_element_type=F32)
            for k, q in enumerate(chips):
                base = acts_in[span(q, 2), :, span(g, LANES)].reshape(BLOCK, LANES).astype(F32)
                mine = delta[k * BLOCK : (k + 1) * BLOCK]
                send_out[g, span(q, 2)] = (base + mine).astype(BF16).reshape(2, ROWS, LANES)
            for hops, q in zip(pair, chips):
                if hops == 0:
                    out_copy(g)(sibling, e).start()
                    hand_copy(g, e, True).start()
                else:
                    out_copy(g)(2 * q + 1 - c, e).start()
                    out_copy(g)(2 * q + c, e).start()


    def forward(g, devices):
        for device in devices:
            out_copy(g)(device, device).wait_recv()
            hand_copy(g, device, False).start()

    out_part(0)
    forward(0, arrivals[:5])
    out_part(1)
    forward(0, arrivals[5:])
    out_part(2)
    forward(1, arrivals)
    forward(2, arrivals)

    def drain_part(g):
        sent(up_copy(g))
        sent(out_copy(g))
        peers(lambda device: hand_copy(g, device, False).wait())
        hand_copy(g, e, True).wait()

    sent(ids_copy)
    gates_copy(c).wait_send()
    sent(part_copy)
    sent(low_copy)
    each(PARTS, drain_part)


def local(acts, index, scores, gain, down, up):
    dma = pltpu.SemaphoreType.DMA
    space = pl.BlockSpec(memory_space=pl.ANY)
    return pl.pallas_call(
        kernel,
        out_shape=jax.ShapeDtypeStruct((ROWS, WIDTH), acts.dtype),
        in_specs=[pl.BlockSpec(memory_space=pltpu.HBM)] * 6,
        out_specs=space,
        scratch_shapes=[
            pltpu.VMEM((ROWS, WIDTH), BF16),
            pltpu.VMEM((GROUP, ROWS, SLICE), BF16),
            pltpu.VMEM((GROUP, ROWS, SLICE), BF16),
            pltpu.VMEM((PARTS, GROUP, ROWS, LANES), BF16),
            pltpu.VMEM((1, SLICE), F32),
            pltpu.VMEM((MB, 2, TOK), jnp.int32),
            pltpu.VMEM((MB, 2, TOK), F32),
            pltpu.VMEM((MB, 8, LANES), F32),
            pltpu.VMEM((LANES, LANES), F32),
            pltpu.VMEM((GROUP, 2, LANES), F32),
            pltpu.VMEM((2, 2, LANES), F32),
            pltpu.VMEM((2, RANK, GROUP * ROWS), F32),
            pltpu.VMEM((GROUP, RANK, BLOCK), F32),
            pltpu.VMEM((GROUP, RANK, BLOCK), BF16),
            pltpu.VMEM((CHIPS, BLOCK, EXPERTS * RANK), BF16),
            pltpu.VMEM((PARTS, GROUP, ROWS, LANES), BF16),
            pltpu.VMEM((PARTS, GROUP, ROWS, LANES), BF16),
            dma((9,)),
        ]
        + [dma((GROUP,))] * 4
        + [dma((PARTS, GROUP))] * 2
        + [dma((GROUP,))] * 2
        + [dma] * 2
        + [dma((GROUP,))] * 4
        + [dma((PARTS, GROUP))] * 4,
        compiler_params=pltpu.CompilerParams(
            collective_id=0, has_side_effects=True, vmem_limit_bytes=60 << 20
        ),
        cost_estimate=pl.CostEstimate(
            flops=4 * 1024 * 1024 * SLICE, bytes_accessed=4 * 786432, transcendentals=0
        ),
        name="relay",
    )(
        acts.reshape(ROWS, WIDTH),
        jnp.swapaxes(index, 2, 3),
        jnp.swapaxes(scores, 2, 3),
        gain,
        down.reshape(ROWS, WIDTH),
        up.reshape(ROWS, WIDTH),
    ).reshape(acts.shape)


def solution(mesh):
    return jax.shard_map(
        local,
        mesh=mesh,
        in_specs=(
            P("section", None, "expert", None),
            P("section", None, "expert", None),
            P("section", None, "expert", None),
            P("section", None),
            P("section", "expert", None, None),
            P("section", "expert", None, None),
        ),
        out_specs=P("section", None, "expert", None),
        check_vma=False,
    )
```

time: 232 us -> 100 us (0.43)
  waiting for transfers between devices: 144 us -> 0 us
  Pallas kernels: 0 us -> 98 us
  local copies, waits for them, and re-layouts: 37.7 us -> 2.06 us
  starting transfers between devices: 27.8 us -> 0 us
  other arithmetic: 13.5 us -> 0 us
  matrix products: 8.06 us -> 0 us
    all_to_all x4 -> x0, waiting for transfers between devices: 122 us -> none  [the longest x2 61.5 us: local(): lax.all_to_all(apply_experts(lax.all_to_all(buffers[step], 'expert', spli...]
    pallas_call x0 -> x1, Pallas kernels: none -> 98 us  [local(): pl.pallas_call(kernel, out_shape=jax.ShapeDtypeStruct((ROWS, WIDTH), acts...]
    all_to_all x4 -> x0, starting transfers between devices: 24.7 us -> none  [the longest x2 16.1 us: local(): lax.all_to_all(buffers[step], 'expert', split_axis=0, concat_axis=0, tile...]
    ppermute x1 -> x0, waiting for transfers between devices: 21.7 us -> none  [shifted(): return lax.ppermute(block, axis, route)]
    convert_element_type x4 -> x0, local copies, waits for them, and re-layouts: 13.7 us -> none  [the longest x2 8.36 us: apply_experts(): return jnp.einsum('nesr,erd->nesd', low_rank, up_projected_rows, preferre...]
    reshape x4 -> x0, local copies, waits for them, and re-layouts: 11 us -> none  [the longest x2 7.12 us: local(): flat_back = returned.reshape(total_slots, last_width)]
    dot_general x2 -> x0, matrix products: 8.06 us -> none  [apply_experts(): jnp.einsum('nesr,erd->nesd', low_rank, up_projected_rows, preferred_eleme...]
    gather x4 -> x0, local copies, waits for them, and re-layouts: 7.33 us -> none  [the longest x2 5.29 us: fill_slots(): picked = jnp.take(normed, tokens_of, axis=0)]
  transfers between devices with their start and end apart: 5 -> 0, of which waited for: 5 -> 0; matrix products, arithmetic and copies ran while one was open for 14% -> 0% of each run, Pallas kernels for 0% -> 0%
where the time goes in v2:
time: 100 us
  Pallas kernels  98 us (98%)
  local copies, waits for them, and re-layouts  2.06 us (2%)
    pallas_call x1, Pallas kernels, local(): pl.pallas_call(kernel, out_shape=jax.ShapeDtypeStruct((ROWS, WIDTH), acts...  98 us
    unnamed x1, local copies, waits for them, and re-layouts  2.06 us

profile of v2, /device:TPU:1, one launch (start us, length us, event | category | flops | bytes accessed | tf_op | source)
XLA Modules:
  0.0 100.1 jit_solution(10611899734259035087)
XLA Ops:
  0.0 98.0 %relay.1 = bf16[64,6144]{1,0:T(8,128)(2,1)} custom-call(bf16[64,6144]{1,0:T(8,128)(2,1)} %bitcast.7, s32[1,2,2,32]{3,2,1,0:T(2,128)} %bitcast.10, f32[1,2,2,32]{3,2,1,0:T(2,128)} %bitcast.11, f32[1,6144]{1,0:T(1,128)} %gain.1, bf16[64,6144]{1,0:T(8,128)(2,1)} %bitcast.8, bf16[64,6144]{1,0:T(8,128)(2,1)} %bitcast.9), custom_call_target="tpu_custom_call" | custom-call | flops 1610612736 | bytes 3145728 | tf_op jit(solution)/shard_map/relay/pallas_call | solution.py:352
  98.0 2.1 %copy.8 = bf16[1,2,32,6144]{3,2,1,0:T(8,128)(2,1)} copy(bf16[1,2,32,6144]{3,2,1,0:T(8,128)(2,1)} %bitcast.6) | data formatting | bytes 1572864

commit v3 on v2

--- a/solution.py
+++ b/solution.py
@@ -54,6 +54,11 @@
     red,
     low,
     mixed,
+    mixed_prev,
+    acts_prev,
+    up_prev,
+    ids_prev,
+    low_prev,
     send_out,
     hand,
     local_sem,
@@ -75,6 +80,8 @@
     out_rs,
     hand_ss,
     hand_rs,
+    next_ss,
+    next_rs,
 ):
     s = lax.axis_index("section")
     e = lax.axis_index("expert")
@@ -85,10 +92,6 @@
     s_prev = lax.rem(s + SECTIONS - 1, SECTIONS)
 
     others = [lax.rem(z + hops, CHIPS) * 2 + lax.rem(c + flip, 2) for hops, flip in ORDER]
-    arrivals = [sibling]
-    for hops in NEAR[1:]:
-        other = lax.rem(z + hops, CHIPS) * 2
-        arrivals += [other + 1 - c, other + c]
 
     def span(k, width):
         return pl.ds(pl.multiple_of(k * width, width), width)
@@ -212,6 +215,20 @@
             e,
         )
 
+    def next_copy(k):
+        src, dst = (
+            (acts_in.at[:, :, pl.ds(0, LANES)], acts_prev),
+            (ids_in, ids_prev),
+            (up_in.at[0], up_prev),
+            (low, low_prev),
+        )[k]
+        return remote(src, dst, next_ss.at[k], next_rs.at[k], s_next, e)
+
+    def last_copy(device, slot):
+        return remote(
+            send_out.at[0, device], out.at[:, piece(slot, 0)], out_ss.at[0, device], out_rs.at[0, slot], s, device
+        )
+
     def send(copy):
         peers(lambda device: copy(device, e).start())
 
@@ -240,7 +257,9 @@
     for copy in late:
         copy.wait()
     received(ids_copy)
+    next_copy(1).start()
     received(acts_copy)
+    next_copy(0).start()
     received(down_copy)
 
     def pick_block(n):
@@ -273,6 +292,8 @@
     part_copy(sibling, e).start()
     red[e] = part[c, :, span(z, BLOCK)]
     send(up_copy(1))
+    received(up_copy(0))
+    next_copy(2).start()
     received(part_copy)
     gates_copy(1 - c).wait_recv()
 
@@ -284,66 +305,96 @@
     send(low_copy)
     send(up_copy(2))
     received(low_copy)
-
-
-    def mix_step(q):
-        both = ids_in[2 * q] + ids_in[2 * q + 1]
-        lows = [low[2 * q].astype(F32), low[2 * q + 1].astype(F32)]
-        for g in range(8):
-            pieces = []
-            for h in range(8):
-                expert = float(g * 8 + h)
-                rows = jnp.where(both[1:2] == expert, lows[1], 0.0)
-                pieces.append(jnp.where(both[0:1] == expert, lows[0], rows))
-            tile = jnp.concatenate(pieces, axis=0)
-            mixed[q, :, g * LANES : (g + 1) * LANES] = jnp.transpose(tile).astype(BF16)
-
-    each(CHIPS, mix_step)
-
-    def out_part(g):
-        received(up_copy(g))
-        weights = up_in[g].reshape(EXPERTS * RANK, LANES)
+    next_copy(3).start()
+
+
+    def mix(ids, lows_in, result):
+        def mix_step(q):
+            both = ids[2 * q] + ids[2 * q + 1]
+            lows = [lows_in[2 * q].astype(F32), lows_in[2 * q + 1].astype(F32)]
+            for g in range(8):
+                pieces = []
+                for h in range(8):
+                    expert = float(g * 8 + h)
+                    rows = jnp.where(both[1:2] == expert, lows[1], 0.0)
+                    pieces.append(jnp.where(both[0:1] == expert, lows[0], rows))
+                tile = jnp.concatenate(pieces, axis=0)
+                result[q, :, g * LANES : (g + 1) * LANES] = jnp.transpose(tile).astype(BF16)
+
+        each(CHIPS, mix_step)
+
+    def out_part(g, weights_in, table, base_in, start):
+        weights = weights_in[...].reshape(EXPERTS * RANK, LANES)
         for pair in PAIRS:
             chips = [lax.rem(z + hops, CHIPS) for hops in pair]
-            rows = jnp.concatenate([mixed[q] for q in chips], axis=0)
+            rows = jnp.concatenate([table[q] for q in chips], axis=0)
             delta = jnp.dot(rows, weights, preferred_element_type=F32)
-            for k, q in enumerate(chips):
-                base = acts_in[span(q, 2), :, span(g, LANES)].reshape(BLOCK, LANES).astype(F32)
+            for k, (hops, q) in enumerate(zip(pair, chips)):
+                base = base_in(q).reshape(BLOCK, LANES).astype(F32)
                 mine = delta[k * BLOCK : (k + 1) * BLOCK]
                 send_out[g, span(q, 2)] = (base + mine).astype(BF16).reshape(2, ROWS, LANES)
-            for hops, q in zip(pair, chips):
                 if hops == 0:
-                    out_copy(g)(sibling, e).start()
-                    hand_copy(g, e, True).start()
+                    start(sibling)
                 else:
-                    out_copy(g)(2 * q + 1 - c, e).start()
-                    out_copy(g)(2 * q + c, e).start()
-
+                    start(2 * q + 1 - c)
+                    start(2 * q + c)
+
+    def own_part(g):
+        received(up_copy(g))
+        out_part(
+            g,
+            up_in.at[g],
+            mixed,
+            lambda q: acts_in[span(q, 2), :, g * LANES : (g + 1) * LANES],
+            lambda device: out_copy(g)(device, e).start(),
+        )
+        hand_copy(g, e, True).start()
+
+    arrivals = [sibling]
+    for hops in NEAR[1:]:
+        other = lax.rem(z + hops, CHIPS) * 2
+        arrivals += [other + 1 - c, other + c]
 
     def forward(g, devices):
         for device in devices:
             out_copy(g)(device, device).wait_recv()
             hand_copy(g, device, False).start()
 
-    out_part(0)
-    forward(0, arrivals[:5])
-    out_part(1)
-    forward(0, arrivals[5:])
-    out_part(2)
-    forward(1, arrivals)
+    mix(ids_in, low, mixed)
+    own_part(1)
+    own_part(2)
+    F1 = 5
+    forward(1, arrivals[:F1])
+    for k in range(4):
+        next_copy(k).wait_recv()
+    mix(ids_prev, low_prev, mixed_prev)
+    out_part(
+        0,
+        up_prev,
+        mixed_prev,
+        lambda q: acts_prev[span(q, 2)],
+        lambda device: last_copy(device, e).start(),
+    )
+    last = pltpu.make_async_copy(send_out.at[0, e], out.at[:, piece(e, 0)], local_sem.at[9])
+    last.start()
+    forward(1, arrivals[F1:])
     forward(2, arrivals)
 
-    def drain_part(g):
-        sent(up_copy(g))
+    for g in range(1, PARTS):
         sent(out_copy(g))
         peers(lambda device: hand_copy(g, device, False).wait())
         hand_copy(g, e, True).wait()
-
+    received(last_copy)
+    sent(last_copy)
+    last.wait()
+    for k in range(4):
+        next_copy(k).wait_send()
+    for g in range(PARTS):
+        sent(up_copy(g))
+    gates_copy(c).wait_send()
     sent(ids_copy)
-    gates_copy(c).wait_send()
     sent(part_copy)
     sent(low_copy)
-    each(PARTS, drain_part)
 
 
 def local(acts, index, scores, gain, down, up):
@@ -370,16 +421,22 @@
             pltpu.VMEM((GROUP, RANK, BLOCK), F32),
             pltpu.VMEM((GROUP, RANK, BLOCK), BF16),
             pltpu.VMEM((CHIPS, BLOCK, EXPERTS * RANK), BF16),
+            pltpu.VMEM((CHIPS, BLOCK, EXPERTS * RANK), BF16),
+            pltpu.VMEM((GROUP, ROWS, LANES), BF16),
+            pltpu.VMEM((GROUP, ROWS, LANES), BF16),
+            pltpu.VMEM((GROUP, 2, LANES), F32),
+            pltpu.VMEM((GROUP, RANK, BLOCK), BF16),
             pltpu.VMEM((PARTS, GROUP, ROWS, LANES), BF16),
             pltpu.VMEM((PARTS, GROUP, ROWS, LANES), BF16),
-            dma((9,)),
+            dma((10,)),
         ]
         + [dma((GROUP,))] * 4
         + [dma((PARTS, GROUP))] * 2
         + [dma((GROUP,))] * 2
         + [dma] * 2
         + [dma((GROUP,))] * 4
-        + [dma((PARTS, GROUP))] * 4,
+        + [dma((PARTS, GROUP))] * 4
+        + [dma((4,))] * 2,
         compiler_params=pltpu.CompilerParams(
             collective_id=0, has_side_effects=True, vmem_limit_bytes=60 << 20
         ),

time: 100 us -> 94.9 us (0.949)
  Pallas kernels: 98 us -> 92.6 us
    pallas_call x1, Pallas kernels: 98 us -> 92.6 us  [local(): pl.pallas_call(kernel, out_shape=jax.ShapeDtypeStruct((ROWS, WIDTH), acts...]
where the time goes in v3:
time: 94.9 us; the launch traced here: 94.7 us
  Pallas kernels  92.6 us (98%)
  local copies, waits for them, and re-layouts  2.06 us (2%)
    pallas_call x1, Pallas kernels, local(): pl.pallas_call(kernel, out_shape=jax.ShapeDtypeStruct((ROWS, WIDTH), acts...  92.6 us
    unnamed x1, local copies, waits for them, and re-layouts  2.06 us

profile of v3, /device:TPU:1, one launch (start us, length us, event | category | flops | bytes accessed | tf_op | source)
XLA Modules:
  0.0 94.7 jit_solution(10853841388988496151)
XLA Ops:
  0.0 92.6 %relay.1 = bf16[64,6144]{1,0:T(8,128)(2,1)} custom-call(bf16[64,6144]{1,0:T(8,128)(2,1)} %bitcast.7, s32[1,2,2,32]{3,2,1,0:T(2,128)} %bitcast.10, f32[1,2,2,32]{3,2,1,0:T(2,128)} %bitcast.11, f32[1,6144]{1,0:T(1,128)} %gain.1, bf16[64,6144]{1,0:T(8,128)(2,1)} %bitcast.8, bf16[64,6144]{1,0:T(8,128)(2,1)} %bitcast.9), custom_call_target="tpu_custom_call" | custom-call | flops 1610612736 | bytes 3145728 | tf_op jit(solution)/shard_map/relay/pallas_call | solution.py:403
  92.7 2.1 %copy.8 = bf16[1,2,32,6144]{3,2,1,0:T(8,128)(2,1)} copy(bf16[1,2,32,6144]{3,2,1,0:T(8,128)(2,1)} %bitcast.6) | data formatting | bytes 1572864

commit v4 on v3

--- a/solution.py
+++ b/solution.py
@@ -21,11 +21,10 @@
 PARTS = SLICE // LANES
 BLOCK = 2 * ROWS
 ORDER = (
-    (4, 1), (1, 0), (7, 0), (3, 1), (5, 1), (2, 0), (6, 0), (4, 0),
-    (3, 0), (5, 0), (1, 1), (7, 1), (2, 1), (6, 1), (0, 1),
+    (4, 1), (4, 0), (3, 1), (3, 0), (5, 1), (5, 0), (2, 1), (2, 0),
+    (6, 1), (6, 0), (1, 1), (1, 0), (7, 1), (7, 0), (0, 1),
 )
 NEAR = (0, 1, 7, 2, 6, 3, 5, 4)
-WINDOW = 8
 PAIRS = ((0, 1), (7, 2), (6, 3), (5, 4))
 F32 = jnp.float32
 BF16 = jnp.bfloat16
@@ -240,34 +239,21 @@
 
     gates_copy(c).start()
     send(ids_copy)
-    bulk = [acts_copy(device, e) for device in others] + [down_copy(device, e) for device in others]
-    for k, copy in enumerate(bulk):
-        if k >= WINDOW:
-            bulk[k - WINDOW].wait_send()
-        copy.start()
-    G0 = 3
-    for k, copy in enumerate(bulk[-WINDOW:]):
-        copy.wait_send()
-        for device in others[G0 * k : G0 * (k + 1)]:
-            up_copy(0)(device, e).start()
-    for device in others[G0 * WINDOW :]:
-        up_copy(0)(device, e).start()
-
-
+    send(down_copy)
+    for device in others:
+        down_copy(device, e).wait_send()
+        acts_copy(device, e).start()
     for copy in late:
         copy.wait()
     received(ids_copy)
     next_copy(1).start()
-    received(acts_copy)
-    next_copy(0).start()
     received(down_copy)
 
-    def pick_block(n):
-        tokens = acts_in[span(n, 4)].reshape(2 * BLOCK, SLICE).astype(F32)
+    def pick_block(q):
+        tokens = acts_in[span(q, 2)].reshape(BLOCK, SLICE).astype(F32)
         scaled = (tokens * gain_in[...]).astype(BF16)
-        halves = [ids_in[4 * n + 2 * h] + ids_in[4 * n + 2 * h + 1] for h in range(2)]
-        both = jnp.concatenate(halves, axis=1)
-        picked = [jnp.zeros((RANK, 2 * BLOCK), F32) for _ in range(2)]
+        both = ids_in[2 * q] + ids_in[2 * q + 1]
+        picked = [jnp.zeros((RANK, BLOCK), F32) for _ in range(2)]
         for m in range(4):
             block = down_in[4 * m : 4 * m + 4].reshape(256, SLICE)
             product = lax.dot_general(block, scaled, (((1,), (1,)), ((), ())), preferred_element_type=F32)
@@ -276,33 +262,41 @@
                 for k in range(2):
                     picked[k] = jnp.where(both[k : k + 1] == float(m * 16 + g), rows, picked[k])
         for k in range(2):
-            part[k, :, span(n, 2 * BLOCK)] = picked[k]
-
-    def pick_step(i):
-        n = lax.rem(z // 2 + 1 + i, 4)
-        pick_block(n)
-        for h in range(4):
-            part_copy(4 * n + h, e).start()
-
-    each(3, pick_step)
-    pick_block(z // 2)
-    chip = z + 1 - 2 * lax.rem(z, 2)
-    part_copy(2 * chip, e).start()
-    part_copy(2 * chip + 1, e).start()
+            part[k, :, span(q, BLOCK)] = picked[k].astype(part.dtype)
+
+    def pick_step(j):
+        hops = 4 + ((j + 1) // 2) * (1 - 2 * lax.rem(j, 2))
+        q = lax.rem(z + CHIPS - hops, CHIPS)
+        for device in (2 * q + 1 - c, 2 * q + c):
+            acts_copy(device, device).wait_recv()
+        pick_block(q)
+        for device in (2 * q + 1 - c, 2 * q + c):
+            part_copy(device, e).start()
+            up_copy(0)(device, e).start()
+
+    each(CHIPS - 1, pick_step)
+    acts_copy(sibling, sibling).wait_recv()
+    next_copy(0).start()
+    pick_block(z)
     part_copy(sibling, e).start()
+    up_copy(0)(sibling, e).start()
     red[e] = part[c, :, span(z, BLOCK)]
-    send(up_copy(1))
+    N1 = 11
+    for device in others[:N1]:
+        up_copy(1)(device, e).start()
     received(up_copy(0))
     next_copy(2).start()
     received(part_copy)
     gates_copy(1 - c).wait_recv()
 
-    total = red[0]
+    total = red[0].astype(F32)
     for k in range(1, GROUP):
-        total = total + red[k]
+        total = total + red[k].astype(F32)
     gates = gates_in[0] + gates_in[1]
     low[e] = (total * jnp.where(c == 0, gates[0:1], gates[1:2])).astype(BF16)
     send(low_copy)
+    for device in others[N1:]:
+        up_copy(1)(device, e).start()
     send(up_copy(2))
     received(low_copy)
     next_copy(3).start()
@@ -392,6 +386,7 @@
     for g in range(PARTS):
         sent(up_copy(g))
     gates_copy(c).wait_send()
+    sent(acts_copy)
     sent(ids_copy)
     sent(part_copy)
     sent(low_copy)
@@ -417,8 +412,8 @@
             pltpu.VMEM((LANES, LANES), F32),
             pltpu.VMEM((GROUP, 2, LANES), F32),
             pltpu.VMEM((2, 2, LANES), F32),
-            pltpu.VMEM((2, RANK, GROUP * ROWS), F32),
-            pltpu.VMEM((GROUP, RANK, BLOCK), F32),
+            pltpu.VMEM((2, RANK, GROUP * ROWS), BF16),
+            pltpu.VMEM((GROUP, RANK, BLOCK), BF16),
             pltpu.VMEM((GROUP, RANK, BLOCK), BF16),
             pltpu.VMEM((CHIPS, BLOCK, EXPERTS * RANK), BF16),
             pltpu.VMEM((CHIPS, BLOCK, EXPERTS * RANK), BF16),

time: 94.9 us -> 93 us (0.980)
  Pallas kernels: 92.6 us -> 90.8 us
    pallas_call x1, Pallas kernels: 92.6 us -> 90.8 us  [local(): pl.pallas_call(kernel, out_shape=jax.ShapeDtypeStruct((ROWS, WIDTH), acts...]
where the time goes in v4:
time: 93 us; the launch traced here: 92.9 us
  Pallas kernels  90.8 us (98%)
  local copies, waits for them, and re-layouts  2.06 us (2%)
    pallas_call x1, Pallas kernels, local(): pl.pallas_call(kernel, out_shape=jax.ShapeDtypeStruct((ROWS, WIDTH), acts...  90.8 us
    unnamed x1, local copies, waits for them, and re-layouts  2.06 us

profile of v4, /device:TPU:1, one launch (start us, length us, event | category | flops | bytes accessed | tf_op | source)
XLA Modules:
  0.0 92.9 jit_solution(14003435581560039753)
XLA Ops:
  0.0 90.8 %relay.1 = bf16[64,6144]{1,0:T(8,128)(2,1)} custom-call(bf16[64,6144]{1,0:T(8,128)(2,1)} %bitcast.7, s32[1,2,2,32]{3,2,1,0:T(2,128)} %bitcast.10, f32[1,2,2,32]{3,2,1,0:T(2,128)} %bitcast.11, f32[1,6144]{1,0:T(1,128)} %gain.1, bf16[64,6144]{1,0:T(8,128)(2,1)} %bitcast.8, bf16[64,6144]{1,0:T(8,128)(2,1)} %bitcast.9), custom_call_target="tpu_custom_call" | custom-call | flops 1610612736 | bytes 3145728 | tf_op jit(solution)/shard_map/relay/pallas_call | solution.py:398
  90.8 2.1 %copy.8 = bf16[1,2,32,6144]{3,2,1,0:T(8,128)(2,1)} copy(bf16[1,2,32,6144]{3,2,1,0:T(8,128)(2,1)} %bitcast.6) | data formatting | bytes 1572864

commit v5 on v4

--- a/solution.py
+++ b/solution.py
@@ -21,8 +21,8 @@
 PARTS = SLICE // LANES
 BLOCK = 2 * ROWS
 ORDER = (
-    (4, 1), (4, 0), (3, 1), (3, 0), (5, 1), (5, 0), (2, 1), (2, 0),
-    (6, 1), (6, 0), (1, 1), (1, 0), (7, 1), (7, 0), (0, 1),
+    (0, 1), (4, 1), (4, 0), (3, 1), (3, 0), (5, 1), (5, 0), (2, 1),
+    (2, 0), (6, 1), (6, 0), (1, 1), (1, 0), (7, 1), (7, 0),
 )
 NEAR = (0, 1, 7, 2, 6, 3, 5, 4)
 PAIRS = ((0, 1), (7, 2), (6, 3), (5, 4))
@@ -81,6 +81,8 @@
     hand_rs,
     next_ss,
     next_rs,
+    pass_ss,
+    pass_rs,
 ):
     s = lax.axis_index("section")
     e = lax.axis_index("expert")
@@ -195,6 +197,9 @@
     def low_copy(device, slot):
         return remote(low.at[slot], low.at[slot], low_ss.at[device], low_rs.at[slot], s, device)
 
+    def pass_copy(slot):
+        return remote(low.at[slot], low.at[slot], pass_ss.at[slot], pass_rs.at[slot], s, sibling)
+
     def out_copy(g):
         def copy(device, slot):
             return remote(
@@ -274,18 +279,16 @@
             part_copy(device, e).start()
             up_copy(0)(device, e).start()
 
-    each(CHIPS - 1, pick_step)
     acts_copy(sibling, sibling).wait_recv()
-    next_copy(0).start()
     pick_block(z)
     part_copy(sibling, e).start()
     up_copy(0)(sibling, e).start()
     red[e] = part[c, :, span(z, BLOCK)]
-    N1 = 11
+    each(CHIPS - 1, pick_step)
+    next_copy(0).start()
+    N1 = 15
     for device in others[:N1]:
         up_copy(1)(device, e).start()
-    received(up_copy(0))
-    next_copy(2).start()
     received(part_copy)
     gates_copy(1 - c).wait_recv()
 
@@ -294,14 +297,14 @@
         total = total + red[k].astype(F32)
     gates = gates_in[0] + gates_in[1]
     low[e] = (total * jnp.where(c == 0, gates[0:1], gates[1:2])).astype(BF16)
-    send(low_copy)
+    low_peers = [lax.rem(z + hops, CHIPS) * 2 + c for hops in (4, 3, 5, 2, 6, 1, 7)]
+    for device in low_peers + [sibling]:
+        low_copy(device, e).start()
     for device in others[N1:]:
         up_copy(1)(device, e).start()
     send(up_copy(2))
-    received(low_copy)
-    next_copy(3).start()
-
-
+    received(up_copy(0))
+    next_copy(2).start()
     def mix(ids, lows_in, result):
         def mix_step(q):
             both = ids[2 * q] + ids[2 * q + 1]
@@ -315,12 +318,13 @@
                 tile = jnp.concatenate(pieces, axis=0)
                 result[q, :, g * LANES : (g + 1) * LANES] = jnp.transpose(tile).astype(BF16)
 
-        each(CHIPS, mix_step)
-
-    def out_part(g, weights_in, table, base_in, start):
+        return mix_step
+
+    def out_part(g, weights_in, table, base_in, start, prepare):
         weights = weights_in[...].reshape(EXPERTS * RANK, LANES)
         for pair in PAIRS:
             chips = [lax.rem(z + hops, CHIPS) for hops in pair]
+            prepare(pair, chips)
             rows = jnp.concatenate([table[q] for q in chips], axis=0)
             delta = jnp.dot(rows, weights, preferred_element_type=F32)
             for k, (hops, q) in enumerate(zip(pair, chips)):
@@ -333,7 +337,7 @@
                     start(2 * q + 1 - c)
                     start(2 * q + c)
 
-    def own_part(g):
+    def own_part(g, prepare):
         received(up_copy(g))
         out_part(
             g,
@@ -341,6 +345,7 @@
             mixed,
             lambda q: acts_in[span(q, 2), :, g * LANES : (g + 1) * LANES],
             lambda device: out_copy(g)(device, e).start(),
+            prepare,
         )
         hand_copy(g, e, True).start()
 
@@ -354,20 +359,40 @@
             out_copy(g)(device, device).wait_recv()
             hand_copy(g, device, False).start()
 
-    mix(ids_in, low, mixed)
-    own_part(1)
-    own_part(2)
+    mix_own = mix(ids_in, low, mixed)
+    mix_prev = mix(ids_prev, low_prev, mixed_prev)
+
+    def mix_pair(mix_step, pair):
+        each(2, lambda k: mix_step(lax.rem(z + pair[0] + k * (pair[1] - pair[0]), CHIPS)))
+
+    def low_pair(pair, chips):
+        for hops, q in zip(pair, chips):
+            if hops:
+                pass_copy(2 * q + 1 - c).wait_recv()
+            else:
+                low_copy(sibling, sibling).wait_recv()
+        mix_pair(mix_own, pair)
+
+    def nothing(pair, chips):
+        pass
+
+    for device in low_peers[::-1]:
+        low_copy(device, device).wait_recv()
+        pass_copy(device).start()
+    own_part(1, low_pair)
+    next_copy(3).start()
+    own_part(2, nothing)
     F1 = 5
     forward(1, arrivals[:F1])
     for k in range(4):
         next_copy(k).wait_recv()
-    mix(ids_prev, low_prev, mixed_prev)
     out_part(
         0,
         up_prev,
         mixed_prev,
         lambda q: acts_prev[span(q, 2)],
         lambda device: last_copy(device, e).start(),
+        lambda pair, chips: mix_pair(mix_prev, pair),
     )
     last = pltpu.make_async_copy(send_out.at[0, e], out.at[:, piece(e, 0)], local_sem.at[9])
     last.start()
@@ -389,7 +414,10 @@
     sent(acts_copy)
     sent(ids_copy)
     sent(part_copy)
-    sent(low_copy)
+    for device in low_peers:
+        low_copy(device, e).wait_send()
+        pass_copy(device).wait_send()
+    low_copy(sibling, e).wait_send()
 
 
 def local(acts, index, scores, gain, down, up):
@@ -431,7 +459,8 @@
         + [dma] * 2
         + [dma((GROUP,))] * 4
         + [dma((PARTS, GROUP))] * 4
-        + [dma((4,))] * 2,
+        + [dma((4,))] * 2
+        + [dma((GROUP,))] * 2,
         compiler_params=pltpu.CompilerParams(
             collective_id=0, has_side_effects=True, vmem_limit_bytes=60 << 20
         ),

time: 93 us -> 93.9 us (level)
  no operation moved by 1% of the time
where the time goes in v5:
time: 93.9 us; the launch traced here: 93.7 us
  Pallas kernels  91.6 us (98%)
  local copies, waits for them, and re-layouts  2.06 us (2%)
    pallas_call x1, Pallas kernels, local(): pl.pallas_call(kernel, out_shape=jax.ShapeDtypeStruct((ROWS, WIDTH), acts...  91.6 us
    unnamed x1, local copies, waits for them, and re-layouts  2.06 us

profile of v5, /device:TPU:1, one launch (start us, length us, event | category | flops | bytes accessed | tf_op | source)
XLA Modules:
  0.0 93.7 jit_solution(1016807313694758395)
XLA Ops:
  0.0 91.6 %relay.1 = bf16[64,6144]{1,0:T(8,128)(2,1)} custom-call(bf16[64,6144]{1,0:T(8,128)(2,1)} %bitcast.7, s32[1,2,2,32]{3,2,1,0:T(2,128)} %bitcast.10, f32[1,2,2,32]{3,2,1,0:T(2,128)} %bitcast.11, f32[1,6144]{1,0:T(1,128)} %gain.1, bf16[64,6144]{1,0:T(8,128)(2,1)} %bitcast.8, bf16[64,6144]{1,0:T(8,128)(2,1)} %bitcast.9), custom_call_target="tpu_custom_call" | custom-call | flops 1610612736 | bytes 3145728 | tf_op jit(solution)/shard_map/relay/pallas_call | solution.py:426
  91.6 2.1 %copy.8 = bf16[1,2,32,6144]{3,2,1,0:T(8,128)(2,1)} copy(bf16[1,2,32,6144]{3,2,1,0:T(8,128)(2,1)} %bitcast.6) | data formatting | bytes 1572864
